TPU v7x, 256 devices: a whole 4x4x8 slice. The times are simulated.
256 devices in a mesh: rows: 256 (over y, z, x, core).
Axes of the slice: x: 4, y: 4, z: 8, core: 2. Of those that a mesh axis runs over, the one named last changes fastest.
Arguments:
- sketch: float32 [262144, 512], P('rows'), as said below
- matrix: float32 [262144, 2048], P('rows'), may hold values from -6 to 6
Outputs:
- basis: float32 [262144, 512], P('rows')
- projection: float32 [512, 2048], P(None, 'rows')
Inputs may be any that keep to these rules, and one draw needn't show every extreme that they name: `sketch`: full column rank; column scales differ.
All inputs are finite; a program needn't handle non-finite values.
Results may differ from a plain program's by a relative error of at most 0.00007.
Values sent between devices are 32-bit elements; how exact they have to be, the bound alone decides.
A program may use at most 64 MiB of HBM per device.

v0:
```python
import jax
import jax.numpy as jnp
from jax import lax
from jax.sharding import PartitionSpec as P


def shards(sketch, matrix):
    highest = lax.Precision.HIGHEST
    total_rows = sketch.shape[0] * lax.axis_size("rows")
    root = jnp.sqrt(jnp.float32(total_rows))
    share = matrix.shape[1] // lax.axis_size("rows")
    local_gram = jnp.dot(sketch.T, sketch, precision=highest, preferred_element_type=jnp.float32)
    gram = lax.psum(local_gram, "rows") / total_rows
    lower = jnp.linalg.cholesky(gram)
    basis = lax.linalg.triangular_solve(
        lower, sketch, left_side=False, lower=True, transpose_a=True
    )
    partial_sum = jnp.dot(basis.T, matrix, precision=highest, preferred_element_type=jnp.float32)
    summed = lax.psum(partial_sum, "rows")
    owned = lax.dynamic_slice_in_dim(summed, lax.axis_index("rows") * share, share, 1)
    return (basis, owned / root)


def solution(mesh):
    placed = (P("rows", None), P("rows", None))
    return jax.shard_map(
        shards,
        mesh=mesh,
        in_specs=placed,
        out_specs=(P("rows", None), P(None, "rows")),
        check_vma=False,
    )
```

profile of v0, /device:TPU:1, one launch (start us, length us, event | category | flops | bytes accessed | tf_op | source)
XLA Modules:
  0.0 722.4 jit_solution(2334406464617871478)
XLA Ops:
  7.2 6.7 fusion.36
  13.9 0.6 all-reduce.6.cloned.1.call-start
  14.5 257.8 %all-reduce.4.cloned.1.call-done = f32[512,512]{0,1:T(8,128)} async-done(((f32[512,512]{0,1:T(8,128)}), f32[512,512]{0,1:T(8,128)}) %all-reduce.4.cloned.1.call-update) | async-done | bytes 1048592 | tf_op jit(solution)/shard_map/psum | solution.py:13
  272.3 1.4 broadcast_multiply_fusion
  273.7 0.3 copy.5
  274.1 0.2 fusion.12
  274.3 1.0 copy-done.4
  275.3 11.7 %cholesky.104 = f32[128,128]{1,0:T(8,128)S(1)} custom-call(f32[128,128]{1,0:T(8,128)S(1)} %cholesky.266), custom_call_target="Cholesky" | custom-call | tf_op jit(solution)/shard_map/jit(cholesky)/cholesky | solution.py:14
  287.1 9.8 %custom-call.30 = f32[1,128,128]{1,2,0:T(8,128)S(1)} custom-call(f32[1,128,128]{2,1,0:T(8,128)S(1)} %get-tuple-element.31), custom_call_target="InvertDiagBlocksLowerTriangular" | custom-call | tf_op jit(solution)/shard_map/jit(cholesky)/cholesky | solution.py:14
  296.9 0.1 cholesky.224
  297.0 1.2 constant_dynamic-update-slice_fusion.3
  298.2 1.3 convolution_subtract_fusion.2
  299.5 11.7 %cholesky.217 = f32[128,128]{1,0:T(8,128)S(1)} custom-call(f32[128,128]{1,0:T(8,128)S(1)} %cholesky.270), custom_call_target="Cholesky" | custom-call | tf_op jit(solution)/shard_map/jit(cholesky)/cholesky | solution.py:14
  311.3 10.0 %custom-call.31 = f32[1,128,128]{1,2,0:T(8,128)S(1)} custom-call(f32[1,128,128]{2,1,0:T(8,128)S(1)} %get-tuple-element.28), custom_call_target="InvertDiagBlocksLowerTriangular" | custom-call | tf_op jit(solution)/shard_map/jit(cholesky)/cholesky | solution.py:14
  321.2 0.3 convolution_dynamic-update-slice_fusion
  321.5 1.3 convolution_subtract_fusion.3
  322.8 11.7 %cholesky.238 = f32[128,128]{1,0:T(8,128)S(1)} custom-call(f32[128,128]{1,0:T(8,128)S(1)} %cholesky.275), custom_call_target="Cholesky" | custom-call | tf_op jit(solution)/shard_map/jit(cholesky)/cholesky | solution.py:14
  334.6 0.7 compare_reduce_fusion.1
  335.3 9.8 %custom-call.32 = f32[1,128,128]{1,2,0:T(8,128)S(1)} custom-call(f32[1,128,128]{2,1,0:T(8,128)S(1)} %get-tuple-element.25), custom_call_target="InvertDiagBlocksLowerTriangular" | custom-call | tf_op jit(solution)/shard_map/jit(cholesky)/cholesky | solution.py:14
  345.1 0.2 convolution_dynamic-update-slice_fusion.1
  345.3 1.2 convolution_subtract_fusion.4
  346.6 11.7 %cholesky.255 = f32[128,128]{1,0:T(8,128)S(1)} custom-call(f32[128,128]{1,0:T(8,128)S(1)} %convolution_subtract_fusion.4), custom_call_target="Cholesky" | custom-call | tf_op jit(solution)/shard_map/jit(cholesky)/cholesky | solution.py:14
  358.3 0.6 compare_reduce_fusion
  358.9 0.9 compare_reduce_fusion.2
  362.3 1.1 select_select_fusion
  363.4 14.1 %while.1 = (s32[]{:T(128)}, f32[512,512]{1,0:T(8,128)}, s32[4,2]{0,1:T(2,128)S(1)}, f32[4,128,128]{2,1,0:T(8,128)}, s32[]{:T(128)}) while((s32[]{:T(128)}, f32[512,512]{1,0:T(8,128)}, s32[4,2]{0,1:T(2,128)S(1)}, f32[4,128,128]{2,1,0:T(8,128)}, s32[]{:T(128)}) %tuple.32), condition=%wide.while_cond, body=%wide.while_body.sunk | while | flops 2 | bytes 132705 | solution.py:15
  363.5 0.6 fusion.46
  364.1 2.9 bitcast_dynamic-update-slice_fusion.2
  367.0 0.6 fusion.46
  367.6 2.9 bitcast_dynamic-update-slice_fusion.2
  370.6 0.6 fusion.46
  371.2 2.9 bitcast_dynamic-update-slice_fusion.2
  374.1 0.6 fusion.46
  374.7 2.8 bitcast_dynamic-update-slice_fusion.2
  377.5 40.1 %custom-call.33 = f32[4,128,128]{1,2,0:T(8,128)S(1)} custom-call(f32[4,128,128]{2,1,0:T(8,128)} %get-tuple-element.9), custom_call_target="InvertDiagBlocksLowerTriangular" | custom-call | tf_op jit(solution)/shard_map/triangular_solve | solution.py:15
  417.7 0.6 fusion.13
  418.3 1.8 convolution_subtract_fusion.1
  420.2 0.6 fusion.25
  420.8 2.7 convolution_subtract_fusion
  423.5 0.6 fusion.24
  424.2 3.8 fusion.6
  428.0 0.6 fusion.23
  428.6 0.8 copy-done.2
  429.4 17.3 %fusion.34 = f32[512,2048]{0,1:T(8,128)} fusion(f32[1024,2048]{1,0:T(8,128)} %param.3, f32[1024,128]{0,1:T(8,128)S(1)} %fusion.23, f32[1024,128]{0,1:T(8,128)S(1)} %fusion.24, f32[1024,128]{0,1:T(8,128)S(1)} %fusion.25, f32[1024,128]{0,1:T(8,128)S(1)} %bitcast.54), kind=kOutput, calls=%fused_computation.69 | convolution fusion | flops 12886474752 | bytes 14680064 | tf_op jit(solution)/shard_map/dot_general | solution.py:18
  446.7 1.4 pad_maximum_fusion
  448.1 1.8 copy.6
  449.9 264.0 %all-reduce.6.cloned.1.call-done = f32[512,2048]{0,1:T(8,128)} async-done(((f32[512,2048]{0,1:T(8,128)}), f32[512,2048]{0,1:T(8,128)}) %all-reduce.6.cloned.1.call-update) | async-done | bytes 4194320 | tf_op jit(solution)/shard_map/psum | solution.py:19
  713.9 1.3 dynamic-slice_multiply_fusion
  (25 shorter events, 0.6 us)
Async XLA Ops:
  7.2 265.2 %all-reduce.4.cloned.1.call-start = ((), (), s32[]{:S(2)}) async-start(), calls=%async_computation | async-start | bytes 2097152 | tf_op jit(solution)/shard_map/psum | solution.py:13
  13.9 700.0 %all-reduce.6.cloned.1.call-start = ((), (), s32[]{:S(2)}) async-start(), calls=%async_computation.1 | async-start | bytes 8388608 | tf_op jit(solution)/shard_map/psum | solution.py:19
  272.3 1.8 copy-start.3
  274.3 1.0 copy-start.4
  322.8 94.9 %copy-start = (f32[1024,512]{1,0:T(8,128)S(1)}, f32[1024,512]{1,0:T(8,128)}, u32[]{:S(2)}) copy-start(f32[1024,512]{1,0:T(8,128)} %param.2) | copy-start | bytes 6291460
  424.1 4.5 copy-start.1
  428.6 0.8 copy-start.2
Sparse Core Ops, SparseCore 0:
  14.1 258.2 all-reduce.3
  446.8 267.0 all-reduce.5
where the time goes:
time: 727 us; the launch traced here: 722 us
  waiting for transfers between devices  522 us (72%)
  other arithmetic  124 us (17%)
  matrix products  40.3 us (6%)
  local copies, waits for them, and re-layouts  18.2 us (3%)
  between operations  17.1 us (2%)
    psum x1, waiting for transfers between devices, shards(): summed = lax.psum(partial_sum, 'rows')  264 us
    psum x1, waiting for transfers between devices, shards(): gram = lax.psum(local_gram, 'rows') / total_rows  258 us
    another operation x14, other arithmetic, shards(): lower = jnp.linalg.cholesky(gram)  78.8 us
    another operation x4, other arithmetic, shards(): lax.linalg.triangular_solve(lower, sketch, left_side=False, lower=True, t...  42.6 us
    dot_general x1, matrix products, shards(): jnp.dot(basis.T, matrix, precision=highest, preferred_element_type=jnp.fl...  17.3 us
  transfers between devices with their start and end apart: 2, of which 2 were waited for; matrix products, arithmetic and copies ran while one was open for 0% of the time, Pallas kernels for 0%

commit v1 on v0

v1 whole, which is shorter than its diff:
```python
import functools

import jax
import jax.numpy as jnp
from jax import lax
from jax.experimental import pallas as pl
from jax.experimental.pallas import tpu as pltpu
from jax.sharding import PartitionSpec as P

HIGHEST = lax.Precision.HIGHEST
F32, BF16 = jnp.float32, jnp.bfloat16
MESH = pl.DeviceIdType.MESH
RANK = 512
STEP = 32
BLOCKS = [(j, i) for j in range(4) for i in range(j, 4)]
A_ROWS, B_ROWS = 768, 512


def dot(a, b):
    return jnp.dot(a, b, preferred_element_type=F32)


def split2(v):
    hi = v.astype(BF16)
    return hi, (v - hi.astype(F32)).astype(BF16)


def split3(v):
    hi = v.astype(BF16)
    rest = v - hi.astype(F32)
    mid = rest.astype(BF16)
    return hi, mid, (rest - mid.astype(F32)).astype(BF16)


def exchange_kernel(
    s_hbm, m_hbm, g_ref, own_ref,
    s_v, m_v, shi, smid, slo, thi, tmid, tlo,
    p, pa_r1, pb_r1, pa_h1, pb_h1, pa_r2, pb_r2, pa_h2, pb_h2, pa_r3, pb_r3, zb,
    cta, ctb, ca_r1, cb_r1, ca_h1, cb_h1, ca_r2, cb_r2, ca_h2, cb_h2, ca_r3, cb_r3, ch3, c_z,
    ssem, rsem, lsem,
):
    me = lax.axis_index("rows")
    core, x, z, y = me % 2, (me // 2) % 4, (me // 8) % 8, me // 64
    pcore = me + 1 - 2 * core
    xs = [(x + d) % 4 for d in (1, 2, 3)]
    ys = [(y + d) % 4 for d in (1, 2, 3)]
    zs = [(z + d) % 8 for d in range(1, 8)]
    px = [me + (t - x) * 2 for t in xs]
    py = [me + (t - y) * 64 for t in ys]
    pz = [me + (t - z) * 8 for t in zs]

    barrier = pltpu.get_barrier_semaphore()
    for dev in [pcore] + px + py + pz:
        pl.semaphore_signal(barrier, inc=1, device_id=(dev,), device_id_type=MESH)

    load_s = pltpu.make_async_copy(s_hbm, s_v, lsem.at[8])
    load_s.start()
    loads = []
    for j in range(8):
        cols = pl.ds(256 * j, 256)
        load = pltpu.make_async_copy(m_hbm.at[:, cols], m_v.at[:, cols], lsem.at[j])
        load.start()
        loads.append(load)

    sends = []

    def send(src, dst, dev):
        k = len(sends)
        copy = pltpu.make_async_remote_copy(
            src_ref=src, dst_ref=dst, send_sem=ssem.at[k], recv_sem=rsem.at[k],
            device_id=(dev,), device_id_type=MESH,
        )
        copy.start()
        sends.append(copy)
        return copy

    def arrived(copies):
        for copy in copies:
            copy.wait_recv()

    def rows_at(start, size):
        return pl.ds(pl.multiple_of(start, 8), size)

    load_s.wait()
    for r in range(4):
        at = pl.ds(256 * r, 256)
        v = s_v[at, :]
        shi[at, :], smid[at, :], slo[at, :] = split3(v)
        thi[:, at], tmid[:, at], tlo[:, at] = split3(v.T)

    for half in range(2):
        at, cols = pl.ds(256 * half, 256), pl.ds(256 * half, 512 - 256 * half)
        hi, mid, lo = thi[at, :], tmid[at, :], tlo[at, :]
        rhi, rmid, rlo = shi[:, cols], smid[:, cols], slo[:, cols]
        g = (dot(hi, rlo) + dot(lo, rhi) + dot(mid, rmid)) + (dot(hi, rmid) + dot(mid, rhi)) + dot(hi, rhi)
        for k, (j, i) in enumerate(BLOCKS):
            if j // 2 == half:
                a, b = 128 * (j - 2 * half), 128 * (i - 2 * half)
                p[pl.ds(128 * k, 128), :] = g[a:a + 128, b:b + 128]

    pl.semaphore_wait(barrier, 14)

    def project(j):
        loads[j].wait()
        mhi, mlo = split2(m_v[:, pl.ds(256 * j, 256)])
        c = dot(tmid[...], mhi) + dot(thi[...], mlo) + dot(thi[...], mhi)
        ct = c.T
        for t in range(32):
            yy, zz, xx, cc = j // 2, (j % 2) * 4 + t // 8, (t // 2) % 4, t % 2
            tile = ct[8 * t:8 * t + 8, :]
            cta[pl.ds(cc * 1024 + xx * 256 + yy * 64 + zz * 8, 8), :] = tile[:, :256]
            ctb[pl.ds(cc * 1024 + yy * 256 + xx * 64 + zz * 8, 8), :] = tile[:, 256:]

    s1 = [
        send(p.at[rows_at((1 - core) * 384, 384), :], pa_r1, pcore),
        send(p.at[rows_at(A_ROWS + (1 - core) * 256, 256), :], pb_r1, pcore),
    ]
    project(0)
    project(1)
    arrived(s1)
    pa_h1[...] = p[rows_at(core * 384, 384), :] + pa_r1[...]
    pb_h1[...] = p[rows_at(A_ROWS + core * 256, 256), :] + pb_r1[...]
    s2 = [send(pa_h1.at[rows_at(xs[d] * 96, 96), :], pa_r2.at[d], px[d]) for d in range(3)]
    s2 += [send(pb_h1.at[rows_at(ys[d] * 64, 64), :], pb_r2.at[d], py[d]) for d in range(3)]
    project(2)
    project(3)
    arrived(s2)
    pa_h2[...] = pa_h1[rows_at(x * 96, 96), :] + pa_r2[0] + pa_r2[1] + pa_r2[2]
    pb_h2[...] = pb_h1[rows_at(y * 64, 64), :] + pb_r2[0] + pb_r2[1] + pb_r2[2]
    s3 = [send(pa_h2.at[rows_at(ys[d] * 24, 24), :], pa_r3.at[d], py[d]) for d in range(3)]
    s3 += [send(pb_h2.at[rows_at(xs[d] * 16, 16), :], pb_r3.at[d], px[d]) for d in range(3)]
    project(4)
    arrived(s3)
    zb[z, 0:24, :] = pa_h2[rows_at(y * 24, 24), :] + pa_r3[0] + pa_r3[1] + pa_r3[2]
    zb[z, 24:40, :] = pb_h2[rows_at(x * 16, 16), :] + pb_r3[0] + pb_r3[1] + pb_r3[2]
    s4 = [send(zb.at[z], zb.at[z], pz[d]) for d in range(7)]
    project(5)
    project(6)
    arrived(s4)
    total = zb[0]
    for k in range(1, 8):
        total = total + zb[k]
    a3 = rows_at(core * 384 + x * 96 + y * 24, 24)
    b3 = rows_at(A_ROWS + core * 256 + y * 64 + x * 16, 16)
    g_ref[a3, :] = total[:24]
    g_ref[b3, :] = total[24:]
    s5 = [send(g_ref.at[a3, :], g_ref.at[a3, :], py[d]) for d in range(3)]
    s5 += [send(g_ref.at[b3, :], g_ref.at[b3, :], px[d]) for d in range(3)]
    project(7)
    arrived(s5)
    a2 = rows_at(core * 384 + x * 96, 96)
    b2 = rows_at(A_ROWS + core * 256 + y * 64, 64)
    s6 = [send(g_ref.at[a2, :], g_ref.at[a2, :], px[d]) for d in range(3)]
    s6 += [send(g_ref.at[b2, :], g_ref.at[b2, :], py[d]) for d in range(3)]
    c1 = [
        send(cta.at[rows_at((1 - core) * 1024, 1024), :], ca_r1, pcore),
        send(ctb.at[rows_at((1 - core) * 1024, 1024), :], cb_r1, pcore),
    ]
    arrived(s6)
    a1 = rows_at(core * 384, 384)
    b1 = rows_at(A_ROWS + core * 256, 256)
    s7 = [send(g_ref.at[a1, :], g_ref.at[a1, :], pcore), send(g_ref.at[b1, :], g_ref.at[b1, :], pcore)]

    arrived(c1)
    ca_h1[...] = cta[rows_at(core * 1024, 1024), :] + ca_r1[...]
    cb_h1[...] = ctb[rows_at(core * 1024, 1024), :] + cb_r1[...]
    c2 = [send(ca_h1.at[rows_at(xs[d] * 256, 256), :], ca_r2.at[d], px[d]) for d in range(3)]
    c2 += [send(cb_h1.at[rows_at(ys[d] * 256, 256), :], cb_r2.at[d], py[d]) for d in range(3)]
    arrived(s7)
    arrived(c2)
    ca_h2[...] = ca_h1[rows_at(x * 256, 256), :] + ca_r2[0] + ca_r2[1] + ca_r2[2]
    cb_h2[...] = cb_h1[rows_at(y * 256, 256), :] + cb_r2[0] + cb_r2[1] + cb_r2[2]
    c3 = [send(ca_h2.at[rows_at(ys[d] * 64, 64), :], ca_r3.at[d], py[d]) for d in range(3)]
    c3 += [send(cb_h2.at[rows_at(xs[d] * 64, 64), :], cb_r3.at[d], px[d]) for d in range(3)]
    arrived(c3)
    ch3[:, 0:256] = ca_h2[rows_at(y * 64, 64), :] + ca_r3[0] + ca_r3[1] + ca_r3[2]
    ch3[:, 256:512] = cb_h2[rows_at(x * 64, 64), :] + cb_r3[0] + cb_r3[1] + cb_r3[2]
    c4 = [send(ch3.at[rows_at(zs[d] * 8, 8), :], c_z.at[d], pz[d]) for d in range(7)]
    arrived(c4)
    total = ch3[rows_at(z * 8, 8), :]
    for d in range(7):
        total = total + c_z[d]
    own_ref[...] = total
    for copy in sends:
        copy.wait_send()


def exchange(sketch, matrix):
    def f(*shape):
        return pltpu.VMEM(shape, F32)

    def h(*shape):
        return pltpu.VMEM(shape, BF16)

    vmem = pl.BlockSpec(memory_space=pltpu.VMEM)
    rows = sketch.shape[0]
    return pl.pallas_call(
        exchange_kernel,
        out_shape=(jax.ShapeDtypeStruct((A_ROWS + B_ROWS, 128), F32), jax.ShapeDtypeStruct((8, RANK), F32)),
        in_specs=[pl.BlockSpec(memory_space=pl.ANY)] * 2,
        out_specs=(vmem, vmem),
        scratch_shapes=[
            f(rows, RANK), f(*matrix.shape), h(rows, RANK), h(rows, RANK), h(rows, RANK),
            h(RANK, rows), h(RANK, rows), h(RANK, rows),
            f(1280, 128), f(384, 128), f(256, 128), f(384, 128), f(256, 128),
            f(3, 96, 128), f(3, 64, 128), f(96, 128), f(64, 128), f(3, 24, 128), f(3, 16, 128), f(8, 40, 128),
            f(2048, 256), f(2048, 256), f(1024, 256), f(1024, 256), f(1024, 256), f(1024, 256),
            f(3, 256, 256), f(3, 256, 256), f(256, 256), f(256, 256), f(3, 64, 256), f(3, 64, 256),
            f(64, 512), f(7, 8, 512),
            pltpu.SemaphoreType.DMA((56,)), pltpu.SemaphoreType.DMA((56,)), pltpu.SemaphoreType.DMA((9,)),
        ],
        compiler_params=pltpu.CompilerParams(collective_id=0, has_side_effects=True, vmem_limit_bytes=56 << 20),
        cost_estimate=pl.CostEstimate(flops=10_000_000_000, bytes_accessed=10 << 20, transcendentals=0),
        name="exchange",
    )(sketch, matrix)


def invert_factor(w):
    lane = lax.broadcasted_iota(jnp.int32, (8, 128), 1)
    sub = lax.broadcasted_iota(jnp.int32, (8, 128), 0)
    for k in range(RANK // STEP):
        r0 = STEP * k
        lt, off = r0 // 128, r0 % 128
        tiles = [[w[pl.ds(r0 + 8 * t, 8), pl.ds(128 * l, 128)] for l in range(4)] for t in range(4)]
        bc = {}
        for c in range(STEP):
            for t in range(c // 8, 4):
                bc[c, t] = jnp.broadcast_to(tiles[t][lt][:, off + c:off + c + 1], (8, 128))
        inside = (lane >= off) & (lane < off + STEP)
        for t in range(4):
            tiles[t][lt] = jnp.where(inside, (lane - off == sub + 8 * t).astype(F32), tiles[t][lt])
        for j in range(STEP):
            tj, sj = j // 8, j % 8
            r = lax.rsqrt(jnp.broadcast_to(bc[j, tj][sj:sj + 1, :], (8, 128)))
            col = {t: bc[j, t] * r for t in range(tj, 4)}
            row = [jnp.broadcast_to(tiles[tj][l][sj:sj + 1, :], (8, 128)) * r for l in range(4)]
            for c in range(j + 1, STEP):
                scale = jnp.broadcast_to(col[c // 8][c % 8:c % 8 + 1, :], (8, 128))
                for t in range(c // 8, 4):
                    bc[c, t] = bc[c, t] - col[t] * scale
            for t in range(tj, 4):
                if t == tj:
                    below = jnp.where(sub > sj, col[t], 0.0)
                    for l in range(4):
                        tiles[t][l] = jnp.where(sub == sj, row[l], tiles[t][l] - below * row[l])
                else:
                    for l in range(4):
                        tiles[t][l] = tiles[t][l] - col[t] * row[l]
        done = jnp.concatenate([jnp.concatenate(tiles[t], axis=1) for t in range(4)], axis=0)
        w[pl.ds(r0, STEP), :] = done
        rest = RANK - r0 - STEP
        if rest:
            update = jnp.dot(done.T[r0 + STEP:, :], done, precision=HIGHEST, preferred_element_type=F32)
            below = pl.ds(r0 + STEP, rest)
            column = lax.broadcasted_iota(jnp.int32, (rest, RANK), 1)
            w[below, :] = jnp.where((column >= r0) & (column < r0 + STEP), 0.0, w[below, :]) - update
    block_row = lax.broadcasted_iota(jnp.int32, (RANK, RANK), 0) // STEP
    block_column = lax.broadcasted_iota(jnp.int32, (RANK, RANK), 1) // STEP
    w[...] = jnp.where(block_column <= block_row, w[...], 0.0)


def factor_kernel(total_rows, g_ref, own_ref, s_ref, basis_ref, proj_ref, w):
    for k, (j, i) in enumerate(BLOCKS):
        w[pl.ds(128 * j, 128), pl.ds(128 * i, 128)] = g_ref[pl.ds(128 * k, 128), :] * (1.0 / total_rows)
        if i != j:
            w[pl.ds(128 * i, 128), pl.ds(128 * j, 128)] = jnp.zeros((128, 128), F32)
    invert_factor(w)
    wt = w[...].T
    whi, wlo = split2(wt)
    for r in range(4):
        at = pl.ds(256 * r, 256)
        hi, lo = split2(s_ref[at, :])
        basis_ref[at, :] = dot(lo, whi) + dot(hi, wlo) + dot(hi, whi)
    proj_ref[...] = jnp.dot(own_ref[...], wt, precision=HIGHEST, preferred_element_type=F32) * (float(total_rows) ** -0.5)


def factor(total_rows, gram, own, sketch):
    vmem = pl.BlockSpec(memory_space=pltpu.VMEM)
    return pl.pallas_call(
        functools.partial(factor_kernel, total_rows),
        out_shape=(jax.ShapeDtypeStruct(sketch.shape, F32), jax.ShapeDtypeStruct((8, RANK), F32)),
        in_specs=[vmem] * 3,
        out_specs=(vmem, vmem),
        scratch_shapes=[pltpu.VMEM((RANK, RANK), F32)],
        compiler_params=pltpu.CompilerParams(vmem_limit_bytes=40 << 20),
        name="factor",
    )(gram, own, sketch)


def shards(sketch, matrix):
    total_rows = sketch.shape[0] * lax.axis_size("rows")
    gram, own = exchange(sketch, matrix)
    basis, projection = factor(total_rows, gram, own, sketch)
    return basis, projection.T


def solution(mesh):
    placed = (P("rows", None), P("rows", None))
    return jax.shard_map(
        shards,
        mesh=mesh,
        in_specs=placed,
        out_specs=(P("rows", None), P(None, "rows")),
        check_vma=False,
    )
```

time: 727 us -> 88.9 us (0.12)
  waiting for transfers between devices: 522 us -> 0 us
  other arithmetic: 124 us -> 0 us
  Pallas kernels: 0 us -> 86.3 us
  matrix products: 40.3 us -> 0 us
  between operations: 17.1 us -> 0.66 us
  local copies, waits for them, and re-layouts: 18.2 us -> 1.8 us
    psum x2 -> x0, waiting for transfers between devices: 522 us -> none  [the longest x1 264 us: shards(): summed = lax.psum(partial_sum, 'rows')]
    another operation x18 -> x0, other arithmetic: 121 us -> none  [the longest x14 78.8 us: shards(): lower = jnp.linalg.cholesky(gram)]
    pallas_call x0 -> x2, Pallas kernels: none -> 86.3 us  [the longest x1 63.6 us: exchange(): pl.pallas_call(exchange_kernel, out_shape=(jax.ShapeDtypeStruct((A_ROWS +...]
    dot_general x2 -> x0, matrix products: 24 us -> none  [the longest x1 17.3 us: shards(): jnp.dot(basis.T, matrix, precision=highest, preferred_element_type=jnp.fl...]
    another operation x13 -> x0, matrix products: 16.4 us -> none  [the longest x7 10.9 us: shards(): lax.linalg.triangular_solve(lower, sketch, left_side=False, lower=True, t...]
    another operation x17 -> x0, local copies, waits for them, and re-layouts: 14.2 us -> none
  transfers between devices with their start and end apart: 2 -> 0, of which waited for: 2 -> 0; matrix products, arithmetic and copies ran while one was open for 0% -> 0% of each run, Pallas kernels for 0% -> 0%
where the time goes in v1:
time: 88.9 us; the launch traced here: 88.7 us
  Pallas kernels  86.3 us (97%)
  local copies, waits for them, and re-layouts  1.8 us (2%)
    pallas_call x1, Pallas kernels, exchange(): pl.pallas_call(exchange_kernel, out_shape=(jax.ShapeDtypeStruct((A_ROWS +...  63.6 us
    pallas_call x1, Pallas kernels, factor(): pl.pallas_call(functools.partial(factor_kernel, total_rows), out_shape=(j...  22.6 us
    unnamed x6, local copies, waits for them, and re-layouts  1.8 us

profile of v1, /device:TPU:1, one launch (start us, length us, event | category | flops | bytes accessed | tf_op | source)
XLA Modules:
  0.0 88.7 jit_solution(9787403200111860938)
XLA Ops:
  0.6 0.0 copy-start
  0.6 63.6 %exchange.1 = (f32[1280,128]{1,0:T(8,128)}, f32[8,512]{1,0:T(8,128)}) custom-call(f32[1024,512]{1,0:T(8,128)} %s_ref.1, f32[1024,2048]{1,0:T(8,128)} %m_hbm.1), custom_call_target="tpu_custom_call" | custom-call | flops 10000000000 | bytes 10485760 | tf_op jit(solution)/shard_map/exchange/pallas_call | solution.py:197
  64.3 0.0 copy-done
  64.3 0.0 copy-start.1
  64.3 1.1 %copy-done.1 = f32[1280,128]{1,0:T(8,128)S(1)} copy-done((f32[1280,128]{1,0:T(8,128)S(1)}, f32[1280,128]{1,0:T(8,128)}, u32[]{:S(2)}) %copy-start.1) | copy-done | bytes 655384
  65.4 0.0 copy-start.2
  65.4 0.7 copy-done.2
  66.1 22.6 %factor.1 = (f32[1024,512]{1,0:T(8,128)}, f32[8,512]{1,0:T(8,128)}) custom-call(f32[1280,128]{1,0:T(8,128)S(1)} %copy-done.1, f32[8,512]{1,0:T(8,128)S(1)} %copy-done.2, f32[1024,512]{1,0:T(8,128)S(1)} %copy-done), custom_call_target="tpu_custom_call" | custom-call | tf_op jit(solution)/shard_map/factor/pallas_call | solution.py:279
Async XLA Ops:
  0.6 63.6 %copy-start = (f32[1024,512]{1,0:T(8,128)S(1)}, f32[1024,512]{1,0:T(8,128)}, u32[]{:S(2)}) copy-start(f32[1024,512]{1,0:T(8,128)} %s_ref.1) | copy-start | bytes 6291460
  64.3 1.1 %copy-start.1 = (f32[1280,128]{1,0:T(8,128)S(1)}, f32[1280,128]{1,0:T(8,128)}, u32[]{:S(2)}) copy-start(f32[1280,128]{1,0:T(8,128)} %get-tuple-element.6.g_ref) | copy-start | bytes 1966084
  65.4 0.7 copy-start.2

commit v2 on v1

v2 whole, which is shorter than its diff:
```python
import functools

import jax
import jax.numpy as jnp
from jax import lax
from jax.experimental import pallas as pl
from jax.experimental.pallas import tpu as pltpu
from jax.sharding import PartitionSpec as P

HIGHEST = lax.Precision.HIGHEST
F32, BF16 = jnp.float32, jnp.bfloat16
MESH = pl.DeviceIdType.MESH
RANK = 512
STEP = 32
BLOCKS = [(j, i) for j in range(4) for i in range(j, 4)]
A_ROWS, B_ROWS = 768, 512


def dot(a, b):
    return jnp.dot(a, b, preferred_element_type=F32)


def split2(v):
    hi = v.astype(BF16)
    return hi, (v - hi.astype(F32)).astype(BF16)


def split3(v):
    hi = v.astype(BF16)
    rest = v - hi.astype(F32)
    mid = rest.astype(BF16)
    return hi, mid, (rest - mid.astype(F32)).astype(BF16)


def invert_factor(w, after):
    lane = lax.broadcasted_iota(jnp.int32, (8, 128), 1)
    sub = lax.broadcasted_iota(jnp.int32, (8, 128), 0)
    for k in range(RANK // STEP):
        r0 = STEP * k
        lt, off = r0 // 128, r0 % 128
        tiles = [[w[pl.ds(r0 + 8 * t, 8), pl.ds(128 * l, 128)] for l in range(4)] for t in range(4)]
        bc = {}
        for c in range(STEP):
            for t in range(c // 8, 4):
                bc[c, t] = jnp.broadcast_to(tiles[t][lt][:, off + c:off + c + 1], (8, 128))
        inside = (lane >= off) & (lane < off + STEP)
        for t in range(4):
            tiles[t][lt] = jnp.where(inside, (lane - off == sub + 8 * t).astype(F32), tiles[t][lt])
        for j in range(STEP):
            tj, sj = j // 8, j % 8
            r = lax.rsqrt(jnp.broadcast_to(bc[j, tj][sj:sj + 1, :], (8, 128)))
            col = {t: bc[j, t] * r for t in range(tj, 4)}
            row = [jnp.broadcast_to(tiles[tj][l][sj:sj + 1, :], (8, 128)) * r for l in range(4)]
            for c in range(j + 1, STEP):
                scale = jnp.broadcast_to(col[c // 8][c % 8:c % 8 + 1, :], (8, 128))
                for t in range(c // 8, 4):
                    bc[c, t] = bc[c, t] - col[t] * scale
            for t in range(tj, 4):
                if t == tj:
                    below = jnp.where(sub > sj, col[t], 0.0)
                    for l in range(4):
                        tiles[t][l] = jnp.where(sub == sj, row[l], tiles[t][l] - below * row[l])
                else:
                    for l in range(4):
                        tiles[t][l] = tiles[t][l] - col[t] * row[l]
        done = jnp.concatenate([jnp.concatenate(tiles[t], axis=1) for t in range(4)], axis=0)
        w[pl.ds(r0, STEP), :] = done
        rest = RANK - r0 - STEP
        if rest:
            hi, mid, lo = split3(done)
            left = jnp.concatenate([hi, hi, hi, mid, mid, lo], axis=0)[:, r0 + STEP:]
            right = jnp.concatenate([hi, mid, lo, hi, mid, hi], axis=0)
            update = lax.dot_general(left, right, (((0,), (0,)), ((), ())), preferred_element_type=F32)
            below = pl.ds(r0 + STEP, rest)
            column = lax.broadcasted_iota(jnp.int32, (rest, RANK), 1)
            w[below, :] = jnp.where((column >= r0) & (column < r0 + STEP), 0.0, w[below, :]) - update
        if k in after:
            after[k]()
    block_row = lax.broadcasted_iota(jnp.int32, (RANK, RANK), 0) // STEP
    block_column = lax.broadcasted_iota(jnp.int32, (RANK, RANK), 1) // STEP
    w[...] = jnp.where(block_column <= block_row, w[...], 0.0)


def exchange_kernel(
    total_rows, s_hbm, m_hbm, w, own_ref, g_ref,
    s_v, m_v, shi, smid, slo, thi, tmid, tlo,
    p, pa_r1, pb_r1, pa_h1, pb_h1, pa_r2, pb_r2, pa_h2, pb_h2, pa_r3, pb_r3, zb,
    cta, ctb, ca_r1, cb_r1, ca_h1, cb_h1, ca_r2, cb_r2, ca_h2, cb_h2, ca_r3, cb_r3, ch3, c_z,
    ssem, rsem, lsem,
):
    me = lax.axis_index("rows")
    core, x, z, y = me % 2, (me // 2) % 4, (me // 8) % 8, me // 64
    pcore = me + 1 - 2 * core
    xs = [(x + d) % 4 for d in (1, 2, 3)]
    ys = [(y + d) % 4 for d in (1, 2, 3)]
    zs = [(z + d) % 8 for d in range(1, 8)]
    px = [me + (t - x) * 2 for t in xs]
    py = [me + (t - y) * 64 for t in ys]
    pz = [me + (t - z) * 8 for t in zs]

    barrier = pltpu.get_barrier_semaphore()
    for dev in [pcore] + px + py + pz:
        pl.semaphore_signal(barrier, inc=1, device_id=(dev,), device_id_type=MESH)

    load_s = pltpu.make_async_copy(s_hbm, s_v, lsem.at[8])
    load_s.start()
    loads = []
    for j in range(8):
        cols = pl.ds(256 * j, 256)
        load = pltpu.make_async_copy(m_hbm.at[:, cols], m_v.at[:, cols], lsem.at[j])
        load.start()
        loads.append(load)

    sends = []

    def send(src, dst, dev):
        k = len(sends)
        copy = pltpu.make_async_remote_copy(
            src_ref=src, dst_ref=dst, send_sem=ssem.at[k], recv_sem=rsem.at[k],
            device_id=(dev,), device_id_type=MESH,
        )
        copy.start()
        sends.append(copy)
        return copy

    def arrived(copies):
        for copy in copies:
            copy.wait_recv()

    def rows_at(start, size):
        return pl.ds(pl.multiple_of(start, 8), size)

    load_s.wait()
    for r in range(4):
        at = pl.ds(256 * r, 256)
        v = s_v[at, :]
        shi[at, :], smid[at, :], slo[at, :] = split3(v)
        thi[:, at], tmid[:, at], tlo[:, at] = split3(v.T)

    for half in range(2):
        at, cols = pl.ds(256 * half, 256), pl.ds(256 * half, 512 - 256 * half)
        hi, mid, lo = thi[at, :], tmid[at, :], tlo[at, :]
        rhi, rmid, rlo = shi[:, cols], smid[:, cols], slo[:, cols]
        g = (dot(hi, rlo) + dot(lo, rhi) + dot(mid, rmid)) + (dot(hi, rmid) + dot(mid, rhi)) + dot(hi, rhi)
        for k, (j, i) in enumerate(BLOCKS):
            if j // 2 == half:
                a, b = 128 * (j - 2 * half), 128 * (i - 2 * half)
                p[pl.ds(128 * k, 128), :] = g[a:a + 128, b:b + 128]

    pl.semaphore_wait(barrier, 14)

    def project(j):
        loads[j].wait()
        mhi, mlo = split2(m_v[:, pl.ds(256 * j, 256)])
        c = dot(tmid[...], mhi) + dot(thi[...], mlo) + dot(thi[...], mhi)
        ct = c.T
        for t in range(32):
            yy, zz, xx, cc = j // 2, (j % 2) * 4 + t // 8, (t // 2) % 4, t % 2
            tile = ct[8 * t:8 * t + 8, :]
            cta[pl.ds(cc * 1024 + xx * 256 + yy * 64 + zz * 8, 8), :] = tile[:, :256]
            ctb[pl.ds(cc * 1024 + yy * 256 + xx * 64 + zz * 8, 8), :] = tile[:, 256:]

    s1 = [
        send(p.at[rows_at((1 - core) * 384, 384), :], pa_r1, pcore),
        send(p.at[rows_at(A_ROWS + (1 - core) * 256, 256), :], pb_r1, pcore),
    ]
    project(0)
    project(1)
    project(2)
    arrived(s1)
    pa_h1[...] = p[rows_at(core * 384, 384), :] + pa_r1[...]
    pb_h1[...] = p[rows_at(A_ROWS + core * 256, 256), :] + pb_r1[...]
    s2 = [send(pa_h1.at[rows_at(xs[d] * 96, 96), :], pa_r2.at[d], px[d]) for d in range(3)]
    s2 += [send(pb_h1.at[rows_at(ys[d] * 64, 64), :], pb_r2.at[d], py[d]) for d in range(3)]
    project(3)
    project(4)
    project(5)
    arrived(s2)
    pa_h2[...] = pa_h1[rows_at(x * 96, 96), :] + pa_r2[0] + pa_r2[1] + pa_r2[2]
    pb_h2[...] = pb_h1[rows_at(y * 64, 64), :] + pb_r2[0] + pb_r2[1] + pb_r2[2]
    s3 = [send(pa_h2.at[rows_at(ys[d] * 24, 24), :], pa_r3.at[d], py[d]) for d in range(3)]
    s3 += [send(pb_h2.at[rows_at(xs[d] * 16, 16), :], pb_r3.at[d], px[d]) for d in range(3)]
    project(6)
    project(7)
    c1 = [
        send(cta.at[rows_at((1 - core) * 1024, 1024), :], ca_r1, pcore),
        send(ctb.at[rows_at((1 - core) * 1024, 1024), :], cb_r1, pcore),
    ]
    arrived(s3)
    zb[z, 0:24, :] = pa_h2[rows_at(y * 24, 24), :] + pa_r3[0] + pa_r3[1] + pa_r3[2]
    zb[z, 24:40, :] = pb_h2[rows_at(x * 16, 16), :] + pb_r3[0] + pb_r3[1] + pb_r3[2]
    s4 = [send(zb.at[z], zb.at[z], pz[d]) for d in range(7)]
    arrived(s4)
    total = zb[0]
    for k in range(1, 8):
        total = total + zb[k]
    a3 = rows_at(core * 384 + x * 96 + y * 24, 24)
    b3 = rows_at(A_ROWS + core * 256 + y * 64 + x * 16, 16)
    g_ref[a3, :] = total[:24]
    g_ref[b3, :] = total[24:]
    s5 = [send(g_ref.at[a3, :], g_ref.at[a3, :], py[d]) for d in range(3)]
    s5 += [send(g_ref.at[b3, :], g_ref.at[b3, :], px[d]) for d in range(3)]
    arrived(c1)
    ca_h1[...] = cta[rows_at(core * 1024, 1024), :] + ca_r1[...]
    cb_h1[...] = ctb[rows_at(core * 1024, 1024), :] + cb_r1[...]
    arrived(s5)
    a2 = rows_at(core * 384 + x * 96, 96)
    b2 = rows_at(A_ROWS + core * 256 + y * 64, 64)
    s6 = [send(g_ref.at[a2, :], g_ref.at[a2, :], px[d]) for d in range(3)]
    s6 += [send(g_ref.at[b2, :], g_ref.at[b2, :], py[d]) for d in range(3)]
    arrived(s6)
    a1 = rows_at(core * 384, 384)
    b1 = rows_at(A_ROWS + core * 256, 256)
    s7 = [send(g_ref.at[a1, :], g_ref.at[a1, :], pcore), send(g_ref.at[b1, :], g_ref.at[b1, :], pcore)]
    c2 = [send(ca_h1.at[rows_at(xs[d] * 256, 256), :], ca_r2.at[d], px[d]) for d in range(3)]
    c2 += [send(cb_h1.at[rows_at(ys[d] * 256, 256), :], cb_r2.at[d], py[d]) for d in range(3)]
    arrived(s7)
    for k, (j, i) in enumerate(BLOCKS):
        w[pl.ds(128 * j, 128), pl.ds(128 * i, 128)] = g_ref[pl.ds(128 * k, 128), :] * (1.0 / total_rows)
        if i != j:
            w[pl.ds(128 * i, 128), pl.ds(128 * j, 128)] = jnp.zeros((128, 128), F32)

    def second():
        arrived(c2)
        ca_h2[...] = ca_h1[rows_at(x * 256, 256), :] + ca_r2[0] + ca_r2[1] + ca_r2[2]
        cb_h2[...] = cb_h1[rows_at(y * 256, 256), :] + cb_r2[0] + cb_r2[1] + cb_r2[2]
        c3 = [send(ca_h2.at[rows_at(ys[d] * 64, 64), :], ca_r3.at[d], py[d]) for d in range(3)]
        c3 += [send(cb_h2.at[rows_at(xs[d] * 64, 64), :], cb_r3.at[d], px[d]) for d in range(3)]
        moving.append(c3)

    def third():
        arrived(moving.pop())
        ch3[:, 0:256] = ca_h2[rows_at(y * 64, 64), :] + ca_r3[0] + ca_r3[1] + ca_r3[2]
        ch3[:, 256:512] = cb_h2[rows_at(x * 64, 64), :] + cb_r3[0] + cb_r3[1] + cb_r3[2]
        moving.append([send(ch3.at[rows_at(zs[d] * 8, 8), :], c_z.at[d], pz[d]) for d in range(7)])

    moving = []
    invert_factor(w, {9: second, 13: third})
    arrived(moving.pop())
    total = ch3[rows_at(z * 8, 8), :]
    for d in range(7):
        total = total + c_z[d]
    own_ref[...] = total
    for copy in sends:
        copy.wait_send()


def exchange(total_rows, sketch, matrix):
    def f(*shape):
        return pltpu.VMEM(shape, F32)

    def h(*shape):
        return pltpu.VMEM(shape, BF16)

    vmem = pl.BlockSpec(memory_space=pltpu.VMEM)
    rows = sketch.shape[0]
    return pl.pallas_call(
        functools.partial(exchange_kernel, total_rows),
        out_shape=(jax.ShapeDtypeStruct((RANK, RANK), F32), jax.ShapeDtypeStruct((8, RANK), F32)),
        in_specs=[pl.BlockSpec(memory_space=pl.ANY)] * 2,
        out_specs=(vmem, vmem),
        scratch_shapes=[
            f(A_ROWS + B_ROWS, 128),
            f(rows, RANK), f(*matrix.shape), h(rows, RANK), h(rows, RANK), h(rows, RANK),
            h(RANK, rows), h(RANK, rows), h(RANK, rows),
            f(1280, 128), f(384, 128), f(256, 128), f(384, 128), f(256, 128),
            f(3, 96, 128), f(3, 64, 128), f(96, 128), f(64, 128), f(3, 24, 128), f(3, 16, 128), f(8, 40, 128),
            f(2048, 256), f(2048, 256), f(1024, 256), f(1024, 256), f(1024, 256), f(1024, 256),
            f(3, 256, 256), f(3, 256, 256), f(256, 256), f(256, 256), f(3, 64, 256), f(3, 64, 256),
            f(64, 512), f(7, 8, 512),
            pltpu.SemaphoreType.DMA((56,)), pltpu.SemaphoreType.DMA((56,)), pltpu.SemaphoreType.DMA((9,)),
        ],
        compiler_params=pltpu.CompilerParams(collective_id=0, has_side_effects=True, vmem_limit_bytes=40 << 20),
        cost_estimate=pl.CostEstimate(flops=10_000_000_000, bytes_accessed=10 << 20, transcendentals=0),
        name="exchange",
    )(sketch, matrix)


def finish_kernel(total_rows, s_ref, w_ref, own_ref, basis_ref, proj_ref, whi, wlo):
    @pl.when(pl.program_id(0) == 0)
    def _():
        wt = w_ref[...].T
        whi[...], wlo[...] = split2(wt)
        proj_ref[...] = jnp.dot(own_ref[...], wt, precision=HIGHEST, preferred_element_type=F32) * (float(total_rows) ** -0.5)

    hi, lo = split2(s_ref[...])
    basis_ref[...] = dot(lo, whi[...]) + dot(hi, wlo[...]) + dot(hi, whi[...])


def finish(total_rows, sketch, w, own):
    block = pl.BlockSpec((256, RANK), lambda r: (r, 0))
    vmem = pl.BlockSpec(memory_space=pltpu.VMEM)
    return pl.pallas_call(
        functools.partial(finish_kernel, total_rows),
        out_shape=(jax.ShapeDtypeStruct(sketch.shape, F32), jax.ShapeDtypeStruct((8, RANK), F32)),
        grid=(sketch.shape[0] // 256,),
        in_specs=[block, vmem, vmem],
        out_specs=(block, vmem),
        scratch_shapes=[pltpu.VMEM((RANK, RANK), BF16), pltpu.VMEM((RANK, RANK), BF16)],
        compiler_params=pltpu.CompilerParams(vmem_limit_bytes=16 << 20),
        name="finish",
    )(sketch, w, own)


def shards(sketch, matrix):
    total_rows = sketch.shape[0] * lax.axis_size("rows")
    w, own = exchange(total_rows, sketch, matrix)
    basis, projection = finish(total_rows, sketch, w, own)
    return basis, projection.T


def solution(mesh):
    placed = (P("rows", None), P("rows", None))
    return jax.shard_map(
        shards,
        mesh=mesh,
        in_specs=placed,
        out_specs=(P("rows", None), P(None, "rows")),
        check_vma=False,
    )
```

time: 88.9 us -> 76 us (0.85)
  Pallas kernels: 86.3 us -> 70.3 us
  local copies, waits for them, and re-layouts: 1.8 us -> 4.97 us
    pallas_call x2, Pallas kernels: 86.3 us -> 70.3 us  [the longest x1 66.2 us: exchange(): pl.pallas_call(functools.partial(exchange_kernel, total_rows), out_shape=...]
    unnamed x6 -> x4, local copies, waits for them, and re-layouts: 1.8 us -> 4.97 us
where the time goes in v2:
time: 76 us; the launch traced here: 75.9 us
  Pallas kernels  70.3 us (92%)
  local copies, waits for them, and re-layouts  4.97 us (7%)
    pallas_call x1, Pallas kernels, exchange(): pl.pallas_call(functools.partial(exchange_kernel, total_rows), out_shape=...  66.2 us
    unnamed x4, local copies, waits for them, and re-layouts  4.97 us
    pallas_call x1, Pallas kernels, finish(): pl.pallas_call(functools.partial(finish_kernel, total_rows), out_shape=(j...  4.09 us

profile of v2, /device:TPU:1, one launch (start us, length us, event | category | flops | bytes accessed | tf_op | source)
XLA Modules:
  0.0 75.9 jit_solution(3924219143500410865)
XLA Ops:
  0.6 0.0 copy-start
  0.6 1.6 %copy-done = f32[1024,512]{1,0:T(8,128)S(1)} copy-done((f32[1024,512]{1,0:T(8,128)S(1)}, f32[1024,512]{1,0:T(8,128)}, u32[]{:S(2)}) %copy-start) | copy-done | bytes 2097176
  2.2 0.0 copy-start.1
  2.2 3.4 %copy-done.1 = f32[1024,2048]{1,0:T(8,128)S(1)} copy-done((f32[1024,2048]{1,0:T(8,128)S(1)}, f32[1024,2048]{1,0:T(8,128)}, u32[]{:S(2)}) %copy-start.1) | copy-done | bytes 8388632
  5.6 66.2 %exchange.1 = (f32[512,512]{1,0:T(8,128)S(1)}, f32[8,512]{1,0:T(8,128)S(1)}) custom-call(f32[1024,512]{1,0:T(8,128)S(1)} %copy-done, f32[1024,2048]{1,0:T(8,128)S(1)} %copy-done.1), custom_call_target="tpu_custom_call" | custom-call | flops 10000000000 | bytes 10485760 | tf_op jit(solution)/shard_map/exchange/pallas_call | solution.py:257
  71.8 4.1 %finish.1 = (f32[1024,512]{1,0:T(8,128)}, f32[8,512]{1,0:T(8,128)}) custom-call(f32[1024,512]{1,0:T(8,128)S(1)} %copy-done, f32[512,512]{1,0:T(8,128)S(1)} %get-tuple-element.6.w_ref, f32[8,512]{1,0:T(8,128)S(1)} %get-tuple-element.7.own_ref), custom_call_target="tpu_custom_call" | custom-call | tf_op jit(solution)/shard_map/finish/pallas_call | solution.py:293
Async XLA Ops:
  0.6 1.6 %copy-start = (f32[1024,512]{1,0:T(8,128)S(1)}, f32[1024,512]{1,0:T(8,128)}, u32[]{:S(2)}) copy-start(f32[1024,512]{1,0:T(8,128)} %s_ref.1) | copy-start | bytes 6291460
  2.2 3.4 %copy-start.1 = (f32[1024,2048]{1,0:T(8,128)S(1)}, f32[1024,2048]{1,0:T(8,128)}, u32[]{:S(2)}) copy-start(f32[1024,2048]{1,0:T(8,128)} %m_hbm.1) | copy-start | bytes 25165828

commit v3 on v2

v3 whole, which is shorter than its diff:
```python
import functools

import jax
import jax.numpy as jnp
from jax import lax
from jax.experimental import pallas as pl
from jax.experimental.pallas import tpu as pltpu
from jax.sharding import PartitionSpec as P

F32, BF16 = jnp.float32, jnp.bfloat16
MESH = pl.DeviceIdType.MESH
RANK = 512
STEP = 32
BLOCKS = [(j, i) for j in range(1, 4) for i in range(j, 4)] + [(0, i) for i in range(4)]
A_ROWS, B_ROWS = 768, 512
SENDS = 74


def dot(a, b):
    return jnp.dot(a, b, preferred_element_type=F32)


def split2(v):
    hi = v.astype(BF16)
    return hi, (v - hi.astype(F32)).astype(BF16)


def split3(v):
    hi = v.astype(BF16)
    rest = v - hi.astype(F32)
    mid = rest.astype(BF16)
    return hi, mid, (rest - mid.astype(F32)).astype(BF16)


def invert_factor(w, after):
    lane = lax.broadcasted_iota(jnp.int32, (8, 128), 1)
    sub = lax.broadcasted_iota(jnp.int32, (8, 128), 0)
    for k in range(RANK // STEP):
        r0 = STEP * k
        lt, off = r0 // 128, r0 % 128
        tiles = [[w[pl.ds(r0 + 8 * t, 8), pl.ds(128 * l, 128)] for l in range(4)] for t in range(4)]
        bc = {}
        for c in range(STEP):
            for t in range(c // 8, 4):
                bc[c, t] = jnp.broadcast_to(tiles[t][lt][:, off + c:off + c + 1], (8, 128))
        inside = (lane >= off) & (lane < off + STEP)
        for t in range(4):
            tiles[t][lt] = jnp.where(inside, (lane - off == sub + 8 * t).astype(F32), tiles[t][lt])
        for j in range(STEP):
            tj, sj = j // 8, j % 8
            r = lax.rsqrt(jnp.broadcast_to(bc[j, tj][sj:sj + 1, :], (8, 128)))
            col = {t: bc[j, t] * r for t in range(tj, 4)}
            row = [jnp.broadcast_to(tiles[tj][l][sj:sj + 1, :], (8, 128)) * r for l in range(4)]
            for c in range(j + 1, STEP):
                scale = jnp.broadcast_to(col[c // 8][c % 8:c % 8 + 1, :], (8, 128))
                for t in range(c // 8, 4):
                    bc[c, t] = bc[c, t] - col[t] * scale
            for t in range(tj, 4):
                if t == tj:
                    below = jnp.where(sub > sj, col[t], 0.0)
                    for l in range(4):
                        tiles[t][l] = jnp.where(sub == sj, row[l], tiles[t][l] - below * row[l])
                else:
                    for l in range(4):
                        tiles[t][l] = tiles[t][l] - col[t] * row[l]
        done = jnp.concatenate([jnp.concatenate(tiles[t], axis=1) for t in range(4)], axis=0)
        w[pl.ds(r0, STEP), :] = done
        rest = RANK - r0 - STEP
        if rest:
            hi, mid, lo = split3(done)
            left = jnp.concatenate([hi, hi, hi, mid, mid, lo], axis=0)[:, r0 + STEP:]
            right = jnp.concatenate([hi, mid, lo, hi, mid, hi], axis=0)
            update = lax.dot_general(left, right, (((0,), (0,)), ((), ())), preferred_element_type=F32)
            below = pl.ds(r0 + STEP, rest)
            column = lax.broadcasted_iota(jnp.int32, (rest, RANK), 1)
            w[below, :] = jnp.where((column >= r0) & (column < r0 + STEP), 0.0, w[below, :]) - update
        if k in after:
            after[k]()
    block_row = lax.broadcasted_iota(jnp.int32, (RANK, RANK), 0) // STEP
    block_column = lax.broadcasted_iota(jnp.int32, (RANK, RANK), 1) // STEP
    w[...] = jnp.where(block_column <= block_row, w[...], 0.0)


def exchange_kernel(
    total_rows, s_hbm, m_hbm, basis_ref, proj_ref, w, g_ref, whi, wlo,
    s_v, m_v, shi, smid, slo, thi, tmid, tlo,
    p, pa_r1, pb_r1, pa_h1, pb_h1, pa_r2, pb_r2, pa_h2, pb_h2, pa_r3, pb_r3, za, zb,
    ct, c_r1, c_h1, ca_r2, cb_r2, ca_h2, cb_h2, ca_r3, cb_r3, c_h3, c_r4,
    ssem, rsem, lsem,
):
    me = lax.axis_index("rows")
    core, x, z, y = me % 2, (me // 2) % 4, (me // 8) % 8, me // 64
    pcore = me + 1 - 2 * core
    xs = [(x + d) % 4 for d in (1, 2, 3)]
    ys = [(y + d) % 4 for d in (1, 2, 3)]
    zs = [(z + d) % 8 for d in range(1, 8)]
    px = [me + (t - x) * 2 for t in xs]
    py = [me + (t - y) * 64 for t in ys]
    pz = [me + (t - z) * 8 for t in zs]

    barrier = pltpu.get_barrier_semaphore()
    for dev in [pcore] + px + py + pz:
        pl.semaphore_signal(barrier, inc=1, device_id=(dev,), device_id_type=MESH)

    load_s = pltpu.make_async_copy(s_hbm, s_v, lsem.at[8])
    load_s.start()
    loads = []
    for j in range(8):
        cols = pl.ds(pl.multiple_of((ys + [y])[j // 2] * 512 + (j % 2) * 256, 256), 256)
        load = pltpu.make_async_copy(m_hbm.at[:, cols], m_v.at[:, pl.ds(256 * j, 256)], lsem.at[j])
        load.start()
        loads.append(load)

    sends = []

    def send(src, dst, dev):
        k = len(sends)
        copy = pltpu.make_async_remote_copy(
            src_ref=src, dst_ref=dst, send_sem=ssem.at[k], recv_sem=rsem.at[k],
            device_id=(dev,), device_id_type=MESH,
        )
        copy.start()
        sends.append(copy)
        return copy

    def arrived(copies):
        for copy in copies:
            copy.wait_recv()

    def rows_at(start, size):
        return pl.ds(pl.multiple_of(start, 8), size)

    load_s.wait()
    for r in range(4):
        at = pl.ds(256 * r, 256)
        v = s_v[at, :]
        shi[at, :], smid[at, :], slo[at, :] = split3(v)
        thi[:, at], tmid[:, at], tlo[:, at] = split3(v.T)

    def gram(half):
        at, cols = pl.ds(256 * half, 256), pl.ds(256 * half, 512 - 256 * half)
        hi, mid, lo = thi[at, :], tmid[at, :], tlo[at, :]
        rhi, rmid, rlo = shi[:, cols], smid[:, cols], slo[:, cols]
        g = (dot(hi, rlo) + dot(lo, rhi) + dot(mid, rmid)) + (dot(hi, rmid) + dot(mid, rhi)) + dot(hi, rhi)
        for k, (j, i) in enumerate(BLOCKS):
            if j // 2 == half:
                a, b = 128 * (j - 2 * half), 128 * (i - 2 * half)
                p[pl.ds(128 * k, 128), :] = g[a:a + 128, b:b + 128]

    def project(j):
        loads[j].wait()
        mhi, mlo = split2(m_v[:, pl.ds(256 * j, 256)])
        c = dot(tmid[...], mhi) + dot(thi[...], mlo) + dot(thi[...], mhi)
        c = c.T
        for t in range(32):
            yy, zz, xx, cc = j // 2, (j % 2) * 4 + t // 8, (t // 2) % 4, t % 2
            ct[pl.ds(cc * 1024 + yy * 256 + xx * 64 + zz * 8, 8), :] = c[8 * t:8 * t + 8, :]

    def a1():
        return [send(p.at[rows_at((1 - core) * 384, 384), :], pa_r1, pcore)]

    def b1():
        return [send(p.at[rows_at(A_ROWS + (1 - core) * 256, 256), :], pb_r1, pcore)]

    def a2():
        pa_h1[...] = p[rows_at(core * 384, 384), :] + pa_r1[...]
        return [send(pa_h1.at[rows_at(xs[d] * 96, 96), :], pa_r2.at[d], px[d]) for d in range(3)]

    def b2():
        pb_h1[...] = p[rows_at(A_ROWS + core * 256, 256), :] + pb_r1[...]
        return [send(pb_h1.at[rows_at(ys[d] * 64, 64), :], pb_r2.at[d], py[d]) for d in range(3)]

    def a3():
        pa_h2[...] = pa_h1[rows_at(x * 96, 96), :] + pa_r2[0] + pa_r2[1] + pa_r2[2]
        return [send(pa_h2.at[rows_at(ys[d] * 24, 24), :], pa_r3.at[d], py[d]) for d in range(3)]

    def b3():
        pb_h2[...] = pb_h1[rows_at(y * 64, 64), :] + pb_r2[0] + pb_r2[1] + pb_r2[2]
        return [send(pb_h2.at[rows_at(xs[d] * 16, 16), :], pb_r3.at[d], px[d]) for d in range(3)]

    def a4():
        za[z] = pa_h2[rows_at(y * 24, 24), :] + pa_r3[0] + pa_r3[1] + pa_r3[2]
        return [send(za.at[z], za.at[z], pz[d]) for d in range(7)]

    def b4():
        zb[z] = pb_h2[rows_at(x * 16, 16), :] + pb_r3[0] + pb_r3[1] + pb_r3[2]
        return [send(zb.at[z], zb.at[z], pz[d]) for d in range(7)]

    def total_of(parts):
        total = parts[0]
        for k in range(1, 8):
            total = total + parts[k]
        return total

    def spread(at, devices):
        return [send(g_ref.at[at, :], g_ref.at[at, :], dev) for dev in devices]

    def a5():
        at = rows_at(core * 384 + x * 96 + y * 24, 24)
        g_ref[at, :] = total_of(za)
        return spread(at, py)

    def b5():
        at = rows_at(A_ROWS + core * 256 + y * 64 + x * 16, 16)
        g_ref[at, :] = total_of(zb)
        return spread(at, px)

    def a6():
        return spread(rows_at(core * 384 + x * 96, 96), px)

    def b6():
        return spread(rows_at(A_ROWS + core * 256 + y * 64, 64), py)

    def a7():
        return spread(rows_at(core * 384, 384), [pcore])

    def b7():
        return spread(rows_at(A_ROWS + core * 256, 256), [pcore])

    def c1(yy):
        return [send(ct.at[rows_at((1 - core) * 1024 + yy * 256, 256), :], c_r1.at[pl.ds(yy * 256, 256), :], pcore)]

    def c_sum(yy):
        at = pl.ds(yy * 256, 256)
        c_h1[at, :] = ct[rows_at(core * 1024 + yy * 256, 256), :] + c_r1[at, :]

    def c2a(yy):
        return [
            send(c_h1.at[rows_at(yy * 256 + xs[d] * 64, 64), pl.ds(0, 256)], ca_r2.at[d, pl.ds(yy * 64, 64), :], px[d])
            for d in range(3)
        ]

    def c2b(d):
        return [send(c_h1.at[pl.ds(d * 256, 256), pl.ds(256, 256)], cb_r2.at[d], py[d])]

    def c3():
        for yy in range(4):
            at = pl.ds(yy * 64, 64)
            own = c_h1[rows_at(yy * 256 + x * 64, 64), pl.ds(0, 256)]
            ca_h2[at, :] = own + ca_r2[0, at, :] + ca_r2[1, at, :] + ca_r2[2, at, :]
        cb_h2[...] = c_h1[pl.ds(768, 256), pl.ds(256, 256)] + cb_r2[0] + cb_r2[1] + cb_r2[2]
        over_y = [send(ca_h2.at[pl.ds(d * 64, 64), :], ca_r3.at[d], py[d]) for d in range(3)]
        over_x = [send(cb_h2.at[rows_at(xs[d] * 64, 64), :], cb_r3.at[d], px[d]) for d in range(3)]
        return over_y + over_x

    def c4():
        c_h3[:, 0:256] = ca_h2[pl.ds(192, 64), :] + ca_r3[0] + ca_r3[1] + ca_r3[2]
        c_h3[:, 256:512] = cb_h2[rows_at(x * 64, 64), :] + cb_r3[0] + cb_r3[1] + cb_r3[2]
        return [send(c_h3.at[rows_at(zs[d] * 8, 8), :], c_r4.at[d], pz[d]) for d in range(7)]

    gram(0)
    pl.semaphore_wait(barrier, 14)
    b = b1()
    gram(1)
    a = a1()
    project(0)
    arrived(b)
    b = b2()
    arrived(a)
    a = a2()
    project(1)
    c = [c1(0)]
    project(2)
    project(3)
    c.append(c1(1))
    arrived(b)
    b = b3()
    arrived(a)
    a = a3()
    project(4)
    project(5)
    c.append(c1(2))
    arrived(b)
    b = b4()
    arrived(a)
    a = a4()
    over = []

    def move(yy):
        arrived(c[yy])
        c_sum(yy)
        over.extend(c2a(yy))
        if yy < 3:
            over.extend(c2b(yy))

    move(0)
    move(1)
    project(6)
    project(7)
    c.append(c1(3))
    arrived(b)
    b = b5()
    arrived(a)
    a = a5()
    arrived(b)
    b = b6()
    arrived(a)
    a = a6()
    move(2)
    move(3)
    arrived(b)
    b = b7()
    arrived(a)
    a = a7()
    for j in range(1, 4):
        w[pl.ds(128 * j, 128), :] = jnp.zeros((128, RANK), F32)
    arrived(b)
    for k in range(6, 10):
        w[pl.ds(0, 128), pl.ds(128 * BLOCKS[k][1], 128)] = g_ref[pl.ds(128 * k, 128), :] * (1.0 / total_rows)

    def take_rest():
        arrived(a)
        for k, (j, i) in enumerate(BLOCKS[:6]):
            at, cols = pl.ds(128 * j, 128), pl.ds(128 * i, 128)
            w[at, cols] = w[at, cols] + g_ref[pl.ds(128 * k, 128), :] * (1.0 / total_rows)

    moving = [over]

    def move_on(stage):
        def run():
            arrived(moving.pop())
            moving.append(stage())
        return run

    invert_factor(w, {3: take_rest, 6: move_on(c3), 11: move_on(c4)})
    def turn(r, carry):
        at = pl.ds(pl.multiple_of(r * 128, 128), 128)
        whi[:, at], wlo[:, at] = split2(w[at, :].T)
        return carry

    lax.fori_loop(0, 4, turn, 0)

    def solve(hi, lo):
        return dot(lo, whi[...]) + dot(hi, wlo[...]) + dot(hi, whi[...])

    def rows_of(r, carry):
        at = pl.ds(pl.multiple_of(256 * r, 256), 256)
        basis_ref[at, :] = solve(shi[at, :], smid[at, :])
        return carry

    lax.fori_loop(0, 4, rows_of, 0)
    arrived(moving.pop())
    total = c_h3[rows_at(z * 8, 8), :]
    for d in range(7):
        total = total + c_r4[d]
    proj_ref[...] = solve(*split2(total * (float(total_rows) ** -0.5)))
    for copy in sends:
        copy.wait_send()


def exchange(total_rows, sketch, matrix):
    def f(*shape):
        return pltpu.VMEM(shape, F32)

    def h(*shape):
        return pltpu.VMEM(shape, BF16)

    vmem = pl.BlockSpec(memory_space=pltpu.VMEM)
    rows = sketch.shape[0]
    return pl.pallas_call(
        functools.partial(exchange_kernel, total_rows),
        out_shape=(jax.ShapeDtypeStruct(sketch.shape, F32), jax.ShapeDtypeStruct((8, RANK), F32)),
        in_specs=[pl.BlockSpec(memory_space=pl.ANY)] * 2,
        out_specs=(vmem, vmem),
        scratch_shapes=[
            f(RANK, RANK), f(A_ROWS + B_ROWS, 128), h(RANK, RANK), h(RANK, RANK),
            f(rows, RANK), f(*matrix.shape), h(rows, RANK), h(rows, RANK), h(rows, RANK),
            h(RANK, rows), h(RANK, rows), h(RANK, rows),
            f(1280, 128), f(384, 128), f(256, 128), f(384, 128), f(256, 128),
            f(3, 96, 128), f(3, 64, 128), f(96, 128), f(64, 128), f(3, 24, 128), f(3, 16, 128), f(8, 24, 128), f(8, 16, 128),
            f(2048, 512), f(1024, 512), f(1024, 512),
            f(3, 256, 256), f(3, 256, 256), f(256, 256), f(256, 256), f(3, 64, 256), f(3, 64, 256),
            f(64, 512), f(7, 8, 512),
            pltpu.SemaphoreType.DMA((SENDS,)), pltpu.SemaphoreType.DMA((SENDS,)), pltpu.SemaphoreType.DMA((9,)),
        ],
        compiler_params=pltpu.CompilerParams(collective_id=0, has_side_effects=True, vmem_limit_bytes=50 << 20),
        cost_estimate=pl.CostEstimate(flops=10_000_000_000, bytes_accessed=10 << 20, transcendentals=0),
        name="exchange",
    )(sketch, matrix)


def shards(sketch, matrix):
    total_rows = sketch.shape[0] * lax.axis_size("rows")
    basis, projection = exchange(total_rows, sketch, matrix)
    return basis, projection.T


def solution(mesh):
    placed = (P("rows", None), P("rows", None))
    return jax.shard_map(
        shards,
        mesh=mesh,
        in_specs=placed,
        out_specs=(P("rows", None), P(None, "rows")),
        check_vma=False,
    )
```

time: 76 us -> 65.9 us (0.87)
  the two profiles are of different devices: /device:TPU:1 before, /device:TPU:2 now
where the time goes in v3:
time: 65.9 us; the launch traced here: 65.8 us
  Pallas kernels  63.2 us (96%)
  local copies, waits for them, and re-layouts  1.93 us (3%)
    pallas_call x1, Pallas kernels, exchange(): pl.pallas_call(functools.partial(exchange_kernel, total_rows), out_shape=...  63.2 us
    unnamed x2, local copies, waits for them, and re-layouts  1.93 us

profile of v3, /device:TPU:2, one launch (start us, length us, event | category | flops | bytes accessed | tf_op | source)
XLA Modules:
  0.0 65.8 jit_solution(13825137554484571484)
XLA Ops:
  0.6 63.2 %exchange.1 = (f32[1024,512]{1,0:T(8,128)S(1)}, f32[8,512]{1,0:T(8,128)S(1)}) custom-call(f32[1024,512]{1,0:T(8,128)} %s_hbm.1, f32[1024,2048]{1,0:T(8,128)} %m_hbm.1), custom_call_target="tpu_custom_call" | custom-call | flops 10000000000 | bytes 10485760 | tf_op jit(solution)/shard_map/exchange/pallas_call | solution.py:360
  63.9 1.3 %copy.6 = f32[1024,512]{1,0:T(8,128)} copy(f32[1024,512]{1,0:T(8,128)S(1)} %get-tuple-element.8) | data formatting | bytes 4194304
  65.2 0.6 copy.7

commit v4 on v3

--- a/solution.py
+++ b/solution.py
@@ -32,10 +32,10 @@
     return hi, mid, (rest - mid.astype(F32)).astype(BF16)
 
 
-def invert_factor(w, after):
+def invert_factor(w, after, always):
     lane = lax.broadcasted_iota(jnp.int32, (8, 128), 1)
     sub = lax.broadcasted_iota(jnp.int32, (8, 128), 0)
-    for k in range(RANK // STEP):
+    def step(k):
         r0 = STEP * k
         lt, off = r0 // 128, r0 % 128
         tiles = [[w[pl.ds(r0 + 8 * t, 8), pl.ds(128 * l, 128)] for l in range(4)] for t in range(4)]
@@ -74,6 +74,8 @@
             below = pl.ds(r0 + STEP, rest)
             column = lax.broadcasted_iota(jnp.int32, (rest, RANK), 1)
             w[below, :] = jnp.where((column >= r0) & (column < r0 + STEP), 0.0, w[below, :]) - update
+    for k in range(RANK // STEP):
+        pl.when(always)(functools.partial(step, k))
         if k in after:
             after[k]()
     block_row = lax.broadcasted_iota(jnp.int32, (RANK, RANK), 0) // STEP
@@ -102,13 +104,16 @@
     for dev in [pcore] + px + py + pz:
         pl.semaphore_signal(barrier, inc=1, device_id=(dev,), device_id_type=MESH)
 
-    load_s = pltpu.make_async_copy(s_hbm, s_v, lsem.at[8])
-    load_s.start()
+    load_s = []
+    for r in range(4):
+        at = pl.ds(256 * r, 256)
+        load = pltpu.make_async_copy(s_hbm.at[at, :], s_v.at[at, :], lsem.at[8 + r])
+        load.start()
+        load_s.append(load)
     loads = []
     for j in range(8):
         cols = pl.ds(pl.multiple_of((ys + [y])[j // 2] * 512 + (j % 2) * 256, 256), 256)
         load = pltpu.make_async_copy(m_hbm.at[:, cols], m_v.at[:, pl.ds(256 * j, 256)], lsem.at[j])
-        load.start()
         loads.append(load)
 
     sends = []
@@ -130,9 +135,12 @@
     def rows_at(start, size):
         return pl.ds(pl.multiple_of(start, 8), size)
 
-    load_s.wait()
     for r in range(4):
         at = pl.ds(256 * r, 256)
+        load_s[r].wait()
+        if r == 3:
+            for load in loads:
+                load.start()
         v = s_v[at, :]
         shi[at, :], smid[at, :], slo[at, :] = split3(v)
         thi[:, at], tmid[:, at], tlo[:, at] = split3(v.T)
@@ -267,13 +275,6 @@
     b = b3()
     arrived(a)
     a = a3()
-    project(4)
-    project(5)
-    c.append(c1(2))
-    arrived(b)
-    b = b4()
-    arrived(a)
-    a = a4()
     over = []
 
     def move(yy):
@@ -284,20 +285,27 @@
             over.extend(c2b(yy))
 
     move(0)
+    project(4)
+    project(5)
+    c.append(c1(2))
+    arrived(b)
+    b = b4()
+    arrived(a)
+    a = a4()
     move(1)
     project(6)
     project(7)
     c.append(c1(3))
+    move(2)
     arrived(b)
     b = b5()
     arrived(a)
     a = a5()
+    move(3)
     arrived(b)
     b = b6()
     arrived(a)
     a = a6()
-    move(2)
-    move(3)
     arrived(b)
     b = b7()
     arrived(a)
@@ -322,7 +330,7 @@
             moving.append(stage())
         return run
 
-    invert_factor(w, {3: take_rest, 6: move_on(c3), 11: move_on(c4)})
+    invert_factor(w, {3: take_rest, 4: move_on(c3), 9: move_on(c4)}, me >= 0)
     def turn(r, carry):
         at = pl.ds(pl.multiple_of(r * 128, 128), 128)
         whi[:, at], wlo[:, at] = split2(w[at, :].T)
@@ -371,7 +379,7 @@
             f(2048, 512), f(1024, 512), f(1024, 512),
             f(3, 256, 256), f(3, 256, 256), f(256, 256), f(256, 256), f(3, 64, 256), f(3, 64, 256),
             f(64, 512), f(7, 8, 512),
-            pltpu.SemaphoreType.DMA((SENDS,)), pltpu.SemaphoreType.DMA((SENDS,)), pltpu.SemaphoreType.DMA((9,)),
+            pltpu.SemaphoreType.DMA((SENDS,)), pltpu.SemaphoreType.DMA((SENDS,)), pltpu.SemaphoreType.DMA((12,)),
         ],
         compiler_params=pltpu.CompilerParams(collective_id=0, has_side_effects=True, vmem_limit_bytes=50 << 20),
         cost_estimate=pl.CostEstimate(flops=10_000_000_000, bytes_accessed=10 << 20, transcendentals=0),

time: 65.9 us -> 63.4 us (0.962)
  the two profiles are of different devices: /device:TPU:2 before, /device:TPU:1 now
where the time goes in v4:
time: 63.4 us; the launch traced here: 62.2 us
  Pallas kernels  59.7 us (94%)
  local copies, waits for them, and re-layouts  1.93 us (3%)
  between operations  0.64 us (1%)
    pallas_call x1, Pallas kernels, exchange(): pl.pallas_call(functools.partial(exchange_kernel, total_rows), out_shape=...  59.7 us
    unnamed x2, local copies, waits for them, and re-layouts  1.93 us

profile of v4, /device:TPU:1, one launch (start us, length us, event | category | flops | bytes accessed | tf_op | source)
XLA Modules:
  0.0 62.2 jit_solution(11762681111291348645)
XLA Ops:
  0.6 59.7 %exchange.1 = (f32[1024,512]{1,0:T(8,128)S(1)}, f32[8,512]{1,0:T(8,128)S(1)}) custom-call(f32[1024,512]{1,0:T(8,128)} %s_hbm.1, f32[1024,2048]{1,0:T(8,128)} %m_hbm.1), custom_call_target="tpu_custom_call" | custom-call | flops 10000000000 | bytes 10485760 | tf_op jit(solution)/shard_map/exchange/pallas_call | solution.py:368
  60.3 1.3 %copy.6 = f32[1024,512]{1,0:T(8,128)} copy(f32[1024,512]{1,0:T(8,128)S(1)} %get-tuple-element.8) | data formatting | bytes 4194304
  61.6 0.6 copy.7
